TPU v7x, 32 devices: a whole 2x2x4 slice. The times are simulated.
32 devices in a mesh: date: 4 (over y, core), tile: 8 (over z, x).
Axes of the slice: x: 2, y: 2, z: 4, core: 2. Of those that a mesh axis runs over, the one named last changes fastest.
Arguments:
- granules: bfloat16 [16, 10, 640, 512], P('date', None, 'tile'), may hold values from -6 to 6
- coef_x: bfloat16 [8, 5, 128, 12], P('tile'), may hold values from -1.75 to 1.75
- coef_y: bfloat16 [8, 5, 16, 12], P('tile'), may hold values from -1.75 to 1.75
- row_offset: int32 [8, 5], P('tile'), may hold values from 0 to 36
- col_offset: int32 [8, 5], P('tile'), may hold values from 0 to 244
- targets: int32 [8, 5], P('tile'), may hold values from -1 to 7, as said below
- mask: int32 [16, 8], P(None, 'tile'), may hold values from 0 to 1, as said below
- smoother: float32 [16, 16], replicated, as said below
Outputs:
- smoothed: float32 [16, 10, 8, 2048], P(None, None, 'tile', 'date')
Inputs may be any that keep to these rules, and one draw needn't show every extreme that they name: `targets`: slot 0 of granule g names tile g; the other slots name, in an order drawn from the seed, each tile other than g within 2 of g in index once, and -1 where such a tile lies beyond the ends. `mask`: every tile has at least one valid date. `smoother`: every entry is positive.
All inputs are finite; a program needn't handle non-finite values.
Results may differ from a plain program's by a relative error of at most 0.0004.
Values sent between devices are 32-bit elements; how exact they have to be, the bound alone decides.
A program may use at most 128 MiB of HBM per device.

v0:
```python
import functools

import jax
import jax.numpy as jnp
from jax import lax
from jax.experimental import pallas as pl
from jax.experimental.pallas import tpu as pltpu
from jax.sharding import PartitionSpec as P

MESH = pl.DeviceIdType.MESH
ROWS = 64


def kernel(dims, tgt_hbm, roff_hbm, coff_hbm, mask_hbm, smoother_hbm, cx_hbm, cy_hbm, g_hbm, out_ref, divisor_ref,
           tgt, roff, coff, mask, smoother, cx_ref, cy_ref, small_sem, g, rx, ymat, high, low, part, recv, final,
           g_sem, send1, recv1, send2, recv2):
    nt, nq, slots, tile_rows, tile_cols, taps, grid_rows, grid_cols, group, rpq, steps, all_dates, bands = dims
    diag, far, side, near, home = range(5)
    tile = lax.axis_index("tile")
    date = lax.axis_index("date")
    turn = 1 - 2 * (tile % 2)
    partner = tile + turn
    ahead = tile - 2 * turn
    behind = tile + 2 * turn
    has_ahead = jnp.logical_and(ahead >= 0, ahead < nt)
    has_behind = jnp.logical_and(behind >= 0, behind < nt)

    def tile_of(slot):
        aim = jnp.where(slot == diag, tile - turn, tile)
        aim = jnp.where(slot == far, ahead, aim)
        aim = jnp.where(slot == side, partner, aim)
        return jnp.where(slot == near, behind, aim)

    def fetch(step):
        return pltpu.make_async_copy(g_hbm.at[pl.ds(2 * step, 2)], g.at[pl.ds(2 * step, 2)], g_sem.at[step])

    pairs = [(tgt_hbm, tgt), (roff_hbm, roff), (coff_hbm, coff), (cy_hbm, cy_ref), (cx_hbm, cx_ref),
             (mask_hbm, mask), (smoother_hbm, smoother)]
    small = [pltpu.make_async_copy(src, dst, small_sem.at[i]) for i, (src, dst) in enumerate(pairs)]
    for copy in small:
        copy.start()
    for step in range(steps):
        fetch(step).start()

    barrier = pltpu.get_barrier_semaphore()
    pl.semaphore_signal(barrier, inc=1, device_id=(date, partner), device_id_type=MESH)
    for c in range(1, nq):
        pl.semaphore_signal(barrier, inc=1, device_id=(lax.rem(date + c, nq), tile), device_id_type=MESH)

    @pl.when(has_ahead)
    def _():
        pl.semaphore_signal(barrier, inc=1, device_id=(date, ahead), device_id_type=MESH)

    @pl.when(has_behind)
    def _():
        pl.semaphore_signal(barrier, inc=1, device_id=(date, behind), device_id_type=MESH)

    for copy in small:
        copy.wait()

    m_count, c_count = slots * tile_rows * group, group * grid_rows
    per_slot = tile_rows * group
    m_e = lax.broadcasted_iota(jnp.int32, (m_count, slots * tile_rows), 0)
    n_e = lax.broadcasted_iota(jnp.int32, (m_count, slots * tile_rows), 1)

    def row_of(m):
        return ((m % per_slot) // (group * rpq)) * rpq + m % rpq

    aimed = jnp.full_like(n_e, -1)
    for k in range(slots):
        aimed = jnp.where(n_e // tile_rows == k, tgt[0, k], aimed)
    pick = jnp.where(jnp.logical_and(row_of(m_e) == n_e % tile_rows, aimed == tile_of(m_e // per_slot)), 1.0, 0.0)
    cy = jnp.dot(pick.astype(jnp.bfloat16), cy_ref[...], preferred_element_type=jnp.float32)
    m = lax.broadcasted_iota(jnp.int32, (m_count, c_count), 0)
    c = lax.broadcasted_iota(jnp.int32, (m_count, c_count), 1)
    shift = jnp.zeros_like(m)
    reach_tile = tile_of(m // per_slot)
    for k in range(slots):
        shift = jnp.where(reach_tile == tgt[0, k], roff[0, k], shift)
    band_c = jnp.zeros_like(c)
    for b in range(1, group):
        band_c = jnp.where(c >= b * grid_rows, b, band_c)
    tap = c - band_c * grid_rows - 2 * row_of(m) - shift
    tap = jnp.where((m // rpq) % group == band_c, tap, -1)
    acc = jnp.zeros((m_count, c_count), jnp.float32)
    for t in range(taps):
        acc = jnp.where(tap == t, cy[:, t:t + 1], acc)
    ymat[...] = acc.astype(jnp.bfloat16)

    def build(r, carry):
        want = tile_of(r)
        coef = jnp.zeros((taps, tile_cols), jnp.float32)
        off = jnp.int32(0)
        for k in range(slots):
            hit = tgt[0, k] == want
            coef = coef + cx_ref[k].astype(jnp.float32) * jnp.where(hit, 1.0, 0.0)
            off = off + jnp.where(hit, coff[0, k], 0)
        row = lax.broadcasted_iota(jnp.int32, (ROWS, tile_cols), 0)
        lane = lax.broadcasted_iota(jnp.int32, (ROWS, tile_cols), 1)
        base = row - 2 * lane - off
        for j in range(grid_cols // ROWS):
            tap = base + j * ROWS
            acc = jnp.zeros((ROWS, tile_cols), jnp.float32)
            for t in range(taps):
                acc = jnp.where(tap == t, coef[t:t + 1, :], acc)
            rx[r, j * ROWS:(j + 1) * ROWS, :] = acc.astype(jnp.bfloat16)
        return carry

    def y_pass(first, count, step):
        rows = ymat[first * per_slot:(first + count) * per_slot, :]
        pair = [
            jnp.dot(rows, g[2 * step + h], preferred_element_type=jnp.float32).reshape(count * nq, 1, 8, grid_cols)
            for h in range(2)
        ]
        both = jnp.concatenate(pair, 1).reshape(count, nq, 16, grid_cols)
        top = both.astype(jnp.bfloat16)
        place = (slice(first, first + count), slice(None), slice(step * 16, (step + 1) * 16), slice(None))
        high[place] = top
        low[place] = (both - top.astype(jnp.float32)).astype(jnp.bfloat16)

    def x_pass(slot, q):
        part[slot, q] = (
            jnp.dot(high[slot, q], rx[slot], preferred_element_type=jnp.float32)
            + jnp.dot(low[slot, q], rx[slot], preferred_element_type=jnp.float32))

    order = [nq // 2] + [s for s in range(1, nq) if s != nq // 2] + [0]
    blocks = [lax.rem(date + s, nq) for s in order]

    def to_tile(slot, i):
        to = {diag: partner if i % 2 else ahead, far: ahead, side: partner, near: behind}[slot]
        q = blocks[i]
        return pltpu.make_async_remote_copy(
            src_ref=part.at[slot, q], dst_ref=recv.at[slot, q], send_sem=send1.at[slot, q], recv_sem=recv1.at[slot, q],
            device_id=(date, to), device_id_type=MESH)

    def to_date(q):
        return pltpu.make_async_remote_copy(
            src_ref=part.at[home, q], dst_ref=final.at[date], send_sem=send2.at[q], recv_sem=recv2.at[date],
            device_id=(q, tile), device_id_type=MESH)

    def from_date(q):
        return pltpu.make_async_remote_copy(
            src_ref=part.at[home, q], dst_ref=final.at[q], send_sem=send2.at[q], recv_sem=recv2.at[q],
            device_id=(q, tile), device_id_type=MESH)

    build(diag, 0)
    for step in range(steps):
        fetch(step).wait()
        y_pass(diag, 1, step)
    peers = nq + jnp.where(has_ahead, 1, 0) + jnp.where(has_behind, 1, 0)
    pl.semaphore_wait(barrier, peers)
    for i in range(nq):
        x_pass(diag, blocks[i])

        @pl.when(has_ahead)
        def _(i=i):
            to_tile(diag, i).start()

    lax.fori_loop(1, slots, build, 0)
    for step in range(steps):
        y_pass(far, slots - 1, step)

    for i in range(nq):
        q = blocks[i]
        x_pass(far, q)

        @pl.when(has_ahead)
        def _(i=i):
            to_tile(far, i).start()

        x_pass(side, q)
        if i % 2:
            to_tile(side, i).start()
        x_pass(near, q)
        if i % 2 == 0:

            @pl.when(has_behind)
            def _(i=i):
                to_tile(near, i).start()

        x_pass(home, q)
        joined = near if i % 2 else side

        @pl.when(has_behind)
        def _(i=i, q=q, joined=joined):
            to_tile(diag, i).wait_recv()
            part[joined, q] = part[joined, q] + recv[diag, q]
            if joined == near:
                to_tile(near, i).start()

        if joined == side:
            to_tile(side, i).start()

    def collect(i):
        q = blocks[i]
        to_tile(side, i).wait_recv()
        part[home, q] = part[home, q] + recv[side, q]

        @pl.when(has_behind)
        def _():
            to_tile(far, i).wait_recv()
            part[home, q] = part[home, q] + recv[far, q]

        @pl.when(has_ahead)
        def _():
            to_tile(near, i).wait_recv()
            part[home, q] = part[home, q] + recv[near, q]

    for i in range(nq - 1):
        collect(i)
        to_date(blocks[i]).start()
    for i in range(nq - 1):
        from_date(blocks[i]).wait_recv()

    rows = bands * rpq
    here = all_dates // nq

    def weight(t, s):
        return smoother[t, s] * mask[0, s].astype(jnp.float32)

    def smooth_others(t, carry):
        total = jnp.zeros((rows, tile_cols), jnp.float32)
        for i in range(nq - 1):
            q = blocks[i]
            for s in range(here):
                total = total + final[q, s * rows:(s + 1) * rows, :] * weight(t, q * here + s)
        out_ref[t] = total
        return carry

    lax.fori_loop(0, all_dates, smooth_others, 0)
    collect(nq - 1)

    def smooth_own(t, carry):
        total = out_ref[t]
        for s in range(here):
            total = total + part[home, date, s * rows:(s + 1) * rows, :] * weight(t, date * here + s)
        divisor = jnp.float32(0.0)
        for s in range(all_dates):
            divisor = divisor + weight(t, s)
        out_ref[t] = total
        divisor_ref[pl.ds(t, 1), :] = jnp.full((1, tile_cols), divisor, jnp.float32)
        return carry

    lax.fori_loop(0, all_dates, smooth_own, 0)

    for i in range(nq):
        to_tile(side, i).wait_send()

        @pl.when(has_ahead)
        def _(i=i):
            to_tile(diag, i).wait_send()
            to_tile(far, i).wait_send()

        @pl.when(has_behind)
        def _(i=i):
            to_tile(near, i).wait_send()

    for i in range(nq - 1):
        to_date(blocks[i]).wait_send()


def body(granules, coef_x, coef_y, row_offset, col_offset, targets, mask, smoother):
    dates, bands, grid_rows, grid_cols = granules.shape
    _, slots, tile_cols, taps = coef_x.shape
    tile_rows = coef_y.shape[2]
    nq, nt = lax.axis_size("date"), lax.axis_size("tile")
    rpq = tile_rows // nq
    group = 8 // rpq
    groups = dates * bands // group
    steps = groups // 2
    all_dates = smoother.shape[0]
    dims = (nt, nq, slots, tile_rows, tile_cols, taps, grid_rows, grid_cols, group, rpq, steps, all_dates, bands)
    block = dates * bands * rpq
    vmem = pl.BlockSpec(memory_space=pltpu.VMEM)
    dma = pltpu.SemaphoreType.DMA
    numerator, divisor = pl.pallas_call(
        functools.partial(kernel, dims),
        out_shape=(jax.ShapeDtypeStruct((all_dates, bands * rpq, tile_cols), jnp.float32),
                   jax.ShapeDtypeStruct((all_dates, tile_cols), jnp.float32)),
        in_specs=[pl.BlockSpec(memory_space=pl.ANY)] * 8,
        out_specs=(vmem, vmem),
        scratch_shapes=[
            pltpu.SMEM((1, slots), jnp.int32),
            pltpu.SMEM((1, slots), jnp.int32),
            pltpu.SMEM((1, slots), jnp.int32),
            pltpu.SMEM((1, all_dates), jnp.int32),
            pltpu.SMEM((all_dates, all_dates), jnp.float32),
            pltpu.VMEM((slots, taps, tile_cols), jnp.bfloat16),
            pltpu.VMEM((slots * tile_rows, taps), jnp.bfloat16),
            dma((7,)),
            pltpu.VMEM((groups, group * grid_rows, grid_cols), jnp.bfloat16),
            pltpu.VMEM((slots, grid_cols, tile_cols), jnp.bfloat16),
            pltpu.VMEM((slots * tile_rows * group, group * grid_rows), jnp.bfloat16),
            pltpu.VMEM((slots, nq, block, grid_cols), jnp.bfloat16),
            pltpu.VMEM((slots, nq, block, grid_cols), jnp.bfloat16),
            pltpu.VMEM((slots, nq, block, tile_cols), jnp.float32),
            pltpu.VMEM((slots, nq, block, tile_cols), jnp.float32),
            pltpu.VMEM((nq, block, tile_cols), jnp.float32),
            dma((steps,)),
            dma((slots, nq)),
            dma((slots, nq)),
            dma((nq,)),
            dma((nq,)),
        ],
        compiler_params=pltpu.CompilerParams(
            collective_id=0, has_side_effects=True, vmem_limit_bytes=60 * 1024 * 1024),
        cost_estimate=pl.CostEstimate(flops=2_000_000_000, bytes_accessed=4_000_000, transcendentals=0),
    )(targets, row_offset, col_offset, mask.reshape(1, all_dates), smoother,
      jnp.transpose(coef_x[0], (0, 2, 1)), coef_y[0].reshape(slots * tile_rows, taps),
      granules.reshape(groups, group * grid_rows, grid_cols))
    smoothed = numerator / divisor[:, None, :]
    return smoothed.reshape(all_dates, bands, 1, rpq * tile_cols)


def solution(mesh):
    return jax.shard_map(
        body,
        mesh=mesh,
        in_specs=(
            P("date", None, "tile", None),
            P("tile", None, None, None),
            P("tile", None, None, None),
            P("tile", None),
            P("tile", None),
            P("tile", None),
            P(None, "tile"),
            P(),
        ),
        out_specs=P(None, None, "tile", "date"),
        check_vma=False,
    )
```

profile of v0, /device:TPU:1, one launch (start us, length us, event | category | flops | bytes accessed | tf_op | source)
XLA Modules:
  0.0 25.2 jit_solution(8387103743937779236)
XLA Ops:
  0.0 23.4 %shard_map.82 = (f32[16,40,128]{2,1,0:T(8,128)}, f32[16,128]{1,0:T(8,128)}) custom-call(s32[1,5]{1,0:T(1,128)} %tgt_hbm.1, s32[1,5]{1,0:T(1,128)} %roff_hbm.1, s32[1,5]{1,0:T(1,128)} %coff_hbm.1, s32[1,16]{1,0:T(1,128)} %bitcast.10, f32[16,16]{1,0:T(8,128)} %smoother_hbm.1, bf16[5,12,128]{2,1,0:T(8,128)(2,1)} %bitcast.8, bf16[80,12]{1,0:T(8,128)(2,1)} %bitcast.9, ...), custom_call_target="tpu_custom_call" | custom-call | flops 2000000000 | bytes 4000000 | tf_op jit(solution)/shard_map/pallas_call | solution.py:276
  23.4 1.7 %broadcast_divide_fusion = f32[16,40,128]{2,1,0:T(8,128)} fusion(f32[16,40,128]{2,1,0:T(8,128)} %get-tuple-element.7, f32[16,128]{1,0:T(8,128)} %get-tuple-element.8), kind=kLoop, calls=%fused_computation | loop fusion | flops 81920 | bytes 663552 | tf_op jit(solution)/shard_map/div | solution.py:311
where the time goes:
time: 25.3 us; the launch traced here: 25.2 us
  Pallas kernels  23.4 us (92%)
  other arithmetic  1.73 us (7%)
    pallas_call x1, Pallas kernels, body(): pl.pallas_call(functools.partial(kernel, dims), out_shape=(jax.ShapeDtype...  23.4 us
    div x1, other arithmetic, body(): smoothed = numerator / divisor[:, None, :]  1.73 us

commit v1 on v0

--- a/solution.py
+++ b/solution.py
@@ -12,7 +12,7 @@
 
 
 def kernel(dims, tgt_hbm, roff_hbm, coff_hbm, mask_hbm, smoother_hbm, cx_hbm, cy_hbm, g_hbm, out_ref, divisor_ref,
-           tgt, roff, coff, mask, smoother, cx_ref, cy_ref, small_sem, g, rx, ymat, high, low, part, recv, final,
+           tgt, roff, coff, mask, smoother, weights, cx_ref, cy_ref, small_sem, g, rx, ymat, parts, part, recv, final,
            g_sem, send1, recv1, send2, recv2):
     nt, nq, slots, tile_rows, tile_cols, taps, grid_rows, grid_cols, group, rpq, steps, all_dates, bands = dims
     diag, far, side, near, home = range(5)
@@ -55,9 +55,6 @@
     def _():
         pl.semaphore_signal(barrier, inc=1, device_id=(date, behind), device_id_type=MESH)
 
-    for copy in small:
-        copy.wait()
-
     m_count, c_count = slots * tile_rows * group, group * grid_rows
     per_slot = tile_rows * group
     m_e = lax.broadcasted_iota(jnp.int32, (m_count, slots * tile_rows), 0)
@@ -66,22 +63,28 @@
     def row_of(m):
         return ((m % per_slot) // (group * rpq)) * rpq + m % rpq
 
-    aimed = jnp.full_like(n_e, -1)
-    for k in range(slots):
-        aimed = jnp.where(n_e // tile_rows == k, tgt[0, k], aimed)
-    pick = jnp.where(jnp.logical_and(row_of(m_e) == n_e % tile_rows, aimed == tile_of(m_e // per_slot)), 1.0, 0.0)
-    cy = jnp.dot(pick.astype(jnp.bfloat16), cy_ref[...], preferred_element_type=jnp.float32)
+    same_row = row_of(m_e) == n_e % tile_rows
+    slot_e = n_e // tile_rows
+    wanted_e = tile_of(m_e // per_slot)
     m = lax.broadcasted_iota(jnp.int32, (m_count, c_count), 0)
     c = lax.broadcasted_iota(jnp.int32, (m_count, c_count), 1)
-    shift = jnp.zeros_like(m)
-    reach_tile = tile_of(m // per_slot)
-    for k in range(slots):
-        shift = jnp.where(reach_tile == tgt[0, k], roff[0, k], shift)
+    wanted = tile_of(m // per_slot)
     band_c = jnp.zeros_like(c)
     for b in range(1, group):
         band_c = jnp.where(c >= b * grid_rows, b, band_c)
-    tap = c - band_c * grid_rows - 2 * row_of(m) - shift
-    tap = jnp.where((m // rpq) % group == band_c, tap, -1)
+    base = c - band_c * grid_rows - 2 * row_of(m)
+    base = jnp.where((m // rpq) % group == band_c, base, -1)
+    for copy in small:
+        copy.wait()
+    aimed = jnp.full_like(n_e, -1)
+    for k in range(slots):
+        aimed = jnp.where(slot_e == k, tgt[0, k], aimed)
+    pick = jnp.where(jnp.logical_and(same_row, aimed == wanted_e), 1.0, 0.0)
+    cy = jnp.dot(pick.astype(jnp.bfloat16), cy_ref[...], preferred_element_type=jnp.float32)
+    shift = jnp.zeros_like(m)
+    for k in range(slots):
+        shift = jnp.where(wanted == tgt[0, k], roff[0, k], shift)
+    tap = base - shift
     acc = jnp.zeros((m_count, c_count), jnp.float32)
     for t in range(taps):
         acc = jnp.where(tap == t, cy[:, t:t + 1], acc)
@@ -114,14 +117,13 @@
         ]
         both = jnp.concatenate(pair, 1).reshape(count, nq, 16, grid_cols)
         top = both.astype(jnp.bfloat16)
-        place = (slice(first, first + count), slice(None), slice(step * 16, (step + 1) * 16), slice(None))
-        high[place] = top
-        low[place] = (both - top.astype(jnp.float32)).astype(jnp.bfloat16)
+        parts[first:first + count, :, 0, step * 16:(step + 1) * 16, :] = top
+        parts[first:first + count, :, 1, step * 16:(step + 1) * 16, :] = (both - top.astype(jnp.float32)).astype(jnp.bfloat16)
 
     def x_pass(slot, q):
-        part[slot, q] = (
-            jnp.dot(high[slot, q], rx[slot], preferred_element_type=jnp.float32)
-            + jnp.dot(low[slot, q], rx[slot], preferred_element_type=jnp.float32))
+        block = part.shape[2]
+        both = jnp.dot(parts[slot, q].reshape(2 * block, grid_cols), rx[slot], preferred_element_type=jnp.float32)
+        part[slot, q] = both[:block] + both[block:]
 
     order = [nq // 2] + [s for s in range(1, nq) if s != nq // 2] + [0]
     blocks = [lax.rem(date + s, nq) for s in order]
@@ -206,42 +208,46 @@
             to_tile(near, i).wait_recv()
             part[home, q] = part[home, q] + recv[near, q]
 
+    def weigh(t, carry):
+        divisor = jnp.float32(0.0)
+        for s in range(all_dates):
+            w = smoother[t, s] * mask[0, s].astype(jnp.float32)
+            weights[t, s] = w
+            divisor = divisor + w
+        divisor_ref[pl.ds(t, 1), :] = jnp.full((1, tile_cols), divisor, jnp.float32)
+        return carry
+
+    lax.fori_loop(0, all_dates, weigh, 0)
+
     for i in range(nq - 1):
         collect(i)
         to_date(blocks[i]).start()
-    for i in range(nq - 1):
-        from_date(blocks[i]).wait_recv()
 
     rows = bands * rpq
     here = all_dates // nq
 
-    def weight(t, s):
-        return smoother[t, s] * mask[0, s].astype(jnp.float32)
-
-    def smooth_others(t, carry):
-        total = jnp.zeros((rows, tile_cols), jnp.float32)
-        for i in range(nq - 1):
-            q = blocks[i]
-            for s in range(here):
-                total = total + final[q, s * rows:(s + 1) * rows, :] * weight(t, q * here + s)
-        out_ref[t] = total
-        return carry
-
-    lax.fori_loop(0, all_dates, smooth_others, 0)
+    def smooth(source, q, first):
+        held = [source[s * rows:(s + 1) * rows, :] for s in range(here)]
+
+        def one(t, carry):
+            total = held[0] * weights[t, q * here]
+            for s in range(1, here):
+                total = total + held[s] * weights[t, q * here + s]
+            out_ref[t] = total if first else out_ref[t] + total
+            return carry
+
+        lax.fori_loop(0, all_dates, one, 0, unroll=4)
+
+    coming = sorted(order[:-1], key=lambda s: order.index(nq - s))
+    for n, s in enumerate(coming[:-1]):
+        q = lax.rem(date + s, nq)
+        from_date(q).wait_recv()
+        smooth(final.at[q], q, n == 0)
     collect(nq - 1)
-
-    def smooth_own(t, carry):
-        total = out_ref[t]
-        for s in range(here):
-            total = total + part[home, date, s * rows:(s + 1) * rows, :] * weight(t, date * here + s)
-        divisor = jnp.float32(0.0)
-        for s in range(all_dates):
-            divisor = divisor + weight(t, s)
-        out_ref[t] = total
-        divisor_ref[pl.ds(t, 1), :] = jnp.full((1, tile_cols), divisor, jnp.float32)
-        return carry
-
-    lax.fori_loop(0, all_dates, smooth_own, 0)
+    smooth(part.at[home, date], date, nq == 2)
+    q = lax.rem(date + coming[-1], nq)
+    from_date(q).wait_recv()
+    smooth(final.at[q], q, False)
 
     for i in range(nq):
         to_tile(side, i).wait_send()
@@ -285,14 +291,14 @@
             pltpu.SMEM((1, slots), jnp.int32),
             pltpu.SMEM((1, all_dates), jnp.int32),
             pltpu.SMEM((all_dates, all_dates), jnp.float32),
+            pltpu.SMEM((all_dates, all_dates), jnp.float32),
             pltpu.VMEM((slots, taps, tile_cols), jnp.bfloat16),
             pltpu.VMEM((slots * tile_rows, taps), jnp.bfloat16),
             dma((7,)),
             pltpu.VMEM((groups, group * grid_rows, grid_cols), jnp.bfloat16),
             pltpu.VMEM((slots, grid_cols, tile_cols), jnp.bfloat16),
             pltpu.VMEM((slots * tile_rows * group, group * grid_rows), jnp.bfloat16),
-            pltpu.VMEM((slots, nq, block, grid_cols), jnp.bfloat16),
-            pltpu.VMEM((slots, nq, block, grid_cols), jnp.bfloat16),
+            pltpu.VMEM((slots, nq, 2, block, grid_cols), jnp.bfloat16),
             pltpu.VMEM((slots, nq, block, tile_cols), jnp.float32),
             pltpu.VMEM((slots, nq, block, tile_cols), jnp.float32),
             pltpu.VMEM((nq, block, tile_cols), jnp.float32),

time: 25.3 us -> 24.3 us (0.960)
  Pallas kernels: 23.4 us -> 22.4 us
    pallas_call x1, Pallas kernels: 23.4 us -> 22.4 us  [body(): pl.pallas_call(functools.partial(kernel, dims), out_shape=(jax.ShapeDtype...]
where the time goes in v1:
time: 24.3 us; the launch traced here: 24.2 us
  Pallas kernels  22.4 us (92%)
  other arithmetic  1.73 us (7%)
    pallas_call x1, Pallas kernels, body(): pl.pallas_call(functools.partial(kernel, dims), out_shape=(jax.ShapeDtype...  22.4 us
    div x1, other arithmetic, body(): smoothed = numerator / divisor[:, None, :]  1.73 us

profile of v1, /device:TPU:1, one launch (start us, length us, event | category | flops | bytes accessed | tf_op | source)
XLA Modules:
  0.0 24.2 jit_solution(4544245342803001885)
XLA Ops:
  0.0 22.4 %shard_map.82 = (f32[16,40,128]{2,1,0:T(8,128)}, f32[16,128]{1,0:T(8,128)}) custom-call(s32[1,5]{1,0:T(1,128)} %tgt_hbm.1, s32[1,5]{1,0:T(1,128)} %roff_hbm.1, s32[1,5]{1,0:T(1,128)} %coff_hbm.1, s32[1,16]{1,0:T(1,128)} %bitcast.10, f32[16,16]{1,0:T(8,128)} %smoother_hbm.1, bf16[5,12,128]{2,1,0:T(8,128)(2,1)} %bitcast.8, bf16[80,12]{1,0:T(8,128)(2,1)} %bitcast.9, ...), custom_call_target="tpu_custom_call" | custom-call | flops 2000000000 | bytes 4000000 | tf_op jit(solution)/shard_map/pallas_call | solution.py:282
  22.4 1.7 %broadcast_divide_fusion = f32[16,40,128]{2,1,0:T(8,128)} fusion(f32[16,40,128]{2,1,0:T(8,128)} %get-tuple-element.7, f32[16,128]{1,0:T(8,128)} %get-tuple-element.8), kind=kLoop, calls=%fused_computation | loop fusion | flops 81920 | bytes 663552 | tf_op jit(solution)/shard_map/div | solution.py:317

commit v2 on v1

--- a/solution.py
+++ b/solution.py
@@ -15,7 +15,7 @@
            tgt, roff, coff, mask, smoother, weights, cx_ref, cy_ref, small_sem, g, rx, ymat, parts, part, recv, final,
            g_sem, send1, recv1, send2, recv2):
     nt, nq, slots, tile_rows, tile_cols, taps, grid_rows, grid_cols, group, rpq, steps, all_dates, bands = dims
-    diag, far, side, near, home = range(5)
+    diag, side, far, near, home = range(5)
     tile = lax.axis_index("tile")
     date = lax.axis_index("date")
     turn = 1 - 2 * (tile % 2)
@@ -146,45 +146,37 @@
             device_id=(q, tile), device_id_type=MESH)
 
     build(diag, 0)
+    build(side, 0)
     for step in range(steps):
         fetch(step).wait()
-        y_pass(diag, 1, step)
+    for step in range(steps):
+        y_pass(diag, 2, step)
     peers = nq + jnp.where(has_ahead, 1, 0) + jnp.where(has_behind, 1, 0)
     pl.semaphore_wait(barrier, peers)
     for i in range(nq):
         x_pass(diag, blocks[i])
 
-        @pl.when(has_ahead)
-        def _(i=i):
+    @pl.when(has_ahead)
+    def _():
+        for i in range(nq):
             to_tile(diag, i).start()
 
-    lax.fori_loop(1, slots, build, 0)
+    for i in range(nq):
+        x_pass(side, blocks[i])
+    for i in range(1, nq, 2):
+        to_tile(side, i).start()
+
+    for r in (far, near, home):
+        build(r, 0)
     for step in range(steps):
-        y_pass(far, slots - 1, step)
-
-    for i in range(nq):
+        y_pass(far, 3, step)
+
+    def relay(i):
+        joined = near if i % 2 else side
         q = blocks[i]
-        x_pass(far, q)
-
-        @pl.when(has_ahead)
-        def _(i=i):
-            to_tile(far, i).start()
-
-        x_pass(side, q)
-        if i % 2:
-            to_tile(side, i).start()
-        x_pass(near, q)
-        if i % 2 == 0:
-
-            @pl.when(has_behind)
-            def _(i=i):
-                to_tile(near, i).start()
-
-        x_pass(home, q)
-        joined = near if i % 2 else side
 
         @pl.when(has_behind)
-        def _(i=i, q=q, joined=joined):
+        def _():
             to_tile(diag, i).wait_recv()
             part[joined, q] = part[joined, q] + recv[diag, q]
             if joined == near:
@@ -192,6 +184,25 @@
 
         if joined == side:
             to_tile(side, i).start()
+
+    relay(0)
+    for i in range(nq):
+        q = blocks[i]
+        for slot in (far, near, home):
+            x_pass(slot, q)
+
+        @pl.when(has_ahead)
+        def _(i=i):
+            to_tile(far, i).start()
+
+        if i % 2 == 0:
+
+            @pl.when(has_behind)
+            def _(i=i):
+                to_tile(near, i).start()
+
+        if i > 0:
+            relay(i)
 
     def collect(i):
         q = blocks[i]

time: 24.3 us -> 24.5 us (level)
  no operation moved by 1% of the time
where the time goes in v2:
time: 24.5 us; the launch traced here: 24.1 us
  Pallas kernels  22.4 us (91%)
  other arithmetic  1.73 us (7%)
    pallas_call x1, Pallas kernels, body(): pl.pallas_call(functools.partial(kernel, dims), out_shape=(jax.ShapeDtype...  22.4 us
    div x1, other arithmetic, body(): smoothed = numerator / divisor[:, None, :]  1.73 us

profile of v2, /device:TPU:1, one launch (start us, length us, event | category | flops | bytes accessed | tf_op | source)
XLA Modules:
  0.0 24.1 jit_solution(2913060689663953800)
XLA Ops:
  0.0 22.4 %shard_map.82 = (f32[16,40,128]{2,1,0:T(8,128)}, f32[16,128]{1,0:T(8,128)}) custom-call(s32[1,5]{1,0:T(1,128)} %tgt_hbm.1, s32[1,5]{1,0:T(1,128)} %roff_hbm.1, s32[1,5]{1,0:T(1,128)} %coff_hbm.1, s32[1,16]{1,0:T(1,128)} %bitcast.10, f32[16,16]{1,0:T(8,128)} %smoother_hbm.1, bf16[5,12,128]{2,1,0:T(8,128)(2,1)} %bitcast.8, bf16[80,12]{1,0:T(8,128)(2,1)} %bitcast.9, ...), custom_call_target="tpu_custom_call" | custom-call | flops 2000000000 | bytes 4000000 | tf_op jit(solution)/shard_map/pallas_call | solution.py:293
  22.4 1.7 %broadcast_divide_fusion = f32[16,40,128]{2,1,0:T(8,128)} fusion(f32[16,40,128]{2,1,0:T(8,128)} %get-tuple-element.7, f32[16,128]{1,0:T(8,128)} %get-tuple-element.8), kind=kLoop, calls=%fused_computation | loop fusion | flops 81920 | bytes 663552 | tf_op jit(solution)/shard_map/div | solution.py:328

commit v3 on v1

--- a/solution.py
+++ b/solution.py
@@ -11,11 +11,16 @@
 ROWS = 64
 
 
+def log(size):
+    assert size & (size - 1) == 0
+    return size.bit_length() - 1
+
+
 def kernel(dims, tgt_hbm, roff_hbm, coff_hbm, mask_hbm, smoother_hbm, cx_hbm, cy_hbm, g_hbm, out_ref, divisor_ref,
            tgt, roff, coff, mask, smoother, weights, cx_ref, cy_ref, small_sem, g, rx, ymat, parts, part, recv, final,
            g_sem, send1, recv1, send2, recv2):
     nt, nq, slots, tile_rows, tile_cols, taps, grid_rows, grid_cols, group, rpq, steps, all_dates, bands = dims
-    diag, far, side, near, home = range(5)
+    diag, side, far, near, home = range(5)
     tile = lax.axis_index("tile")
     date = lax.axis_index("date")
     turn = 1 - 2 * (tile % 2)
@@ -61,19 +66,19 @@
     n_e = lax.broadcasted_iota(jnp.int32, (m_count, slots * tile_rows), 1)
 
     def row_of(m):
-        return ((m % per_slot) // (group * rpq)) * rpq + m % rpq
-
-    same_row = row_of(m_e) == n_e % tile_rows
-    slot_e = n_e // tile_rows
-    wanted_e = tile_of(m_e // per_slot)
+        return ((m & (per_slot - 1)) >> log(group * rpq)) * rpq + (m & (rpq - 1))
+
+    same_row = row_of(m_e) == (n_e & (tile_rows - 1))
+    slot_e = n_e >> log(tile_rows)
+    wanted_e = tile_of(m_e >> log(per_slot))
     m = lax.broadcasted_iota(jnp.int32, (m_count, c_count), 0)
     c = lax.broadcasted_iota(jnp.int32, (m_count, c_count), 1)
-    wanted = tile_of(m // per_slot)
+    wanted = tile_of(m >> log(per_slot))
     band_c = jnp.zeros_like(c)
     for b in range(1, group):
         band_c = jnp.where(c >= b * grid_rows, b, band_c)
     base = c - band_c * grid_rows - 2 * row_of(m)
-    base = jnp.where((m // rpq) % group == band_c, base, -1)
+    base = jnp.where(((m >> log(rpq)) & (group - 1)) == band_c, base, -1)
     for copy in small:
         copy.wait()
     aimed = jnp.full_like(n_e, -1)
@@ -117,20 +122,24 @@
         ]
         both = jnp.concatenate(pair, 1).reshape(count, nq, 16, grid_cols)
         top = both.astype(jnp.bfloat16)
-        parts[first:first + count, :, 0, step * 16:(step + 1) * 16, :] = top
-        parts[first:first + count, :, 1, step * 16:(step + 1) * 16, :] = (both - top.astype(jnp.float32)).astype(jnp.bfloat16)
+        place = pl.ds(pl.multiple_of(step * 16, 16), 16)
+        parts[first:first + count, :, 0, place, :] = top
+        parts[first:first + count, :, 1, place, :] = (both - top.astype(jnp.float32)).astype(jnp.bfloat16)
 
     def x_pass(slot, q):
         block = part.shape[2]
         both = jnp.dot(parts[slot, q].reshape(2 * block, grid_cols), rx[slot], preferred_element_type=jnp.float32)
         part[slot, q] = both[:block] + both[block:]
 
-    order = [nq // 2] + [s for s in range(1, nq) if s != nq // 2] + [0]
-    blocks = [lax.rem(date + s, nq) for s in order]
+    order = list(range(1, nq)) + [0]
+
+    def block_at(i):
+        return lax.rem(date + 1 + i, nq)
 
     def to_tile(slot, i):
-        to = {diag: partner if i % 2 else ahead, far: ahead, side: partner, near: behind}[slot]
-        q = blocks[i]
+        q = block_at(i)
+        to = jnp.where(slot == near, behind, jnp.where(slot == side, partner, ahead))
+        to = jnp.where(jnp.logical_and(slot == diag, i % 2 == 1), partner, to)
         return pltpu.make_async_remote_copy(
             src_ref=part.at[slot, q], dst_ref=recv.at[slot, q], send_sem=send1.at[slot, q], recv_sem=recv1.at[slot, q],
             device_id=(date, to), device_id_type=MESH)
@@ -145,56 +154,70 @@
             src_ref=part.at[home, q], dst_ref=final.at[q], send_sem=send2.at[q], recv_sem=recv2.at[q],
             device_id=(q, tile), device_id_type=MESH)
 
-    build(diag, 0)
+    def y_loop(first, count):
+        def one(step, carry):
+            y_pass(first, count, step)
+            return carry
+
+        lax.fori_loop(0, steps, one, 0, unroll=2 if steps % 2 == 0 else 1)
+
+    lax.fori_loop(diag, side + 1, build, 0)
     for step in range(steps):
         fetch(step).wait()
-        y_pass(diag, 1, step)
+    y_loop(diag, 2)
     peers = nq + jnp.where(has_ahead, 1, 0) + jnp.where(has_behind, 1, 0)
     pl.semaphore_wait(barrier, peers)
-    for i in range(nq):
-        x_pass(diag, blocks[i])
+
+    def phase1(i, carry):
+        q = block_at(i)
+        for slot in (diag, side):
+            x_pass(slot, q)
 
         @pl.when(has_ahead)
-        def _(i=i):
+        def _():
             to_tile(diag, i).start()
 
-    lax.fori_loop(1, slots, build, 0)
-    for step in range(steps):
-        y_pass(far, slots - 1, step)
-
-    for i in range(nq):
-        q = blocks[i]
-        x_pass(far, q)
+        @pl.when(i % 2 == 1)
+        def _():
+            to_tile(side, i).start()
+
+        return carry
+
+    lax.fori_loop(0, nq, phase1, 0)
+
+    lax.fori_loop(far, home + 1, build, 0)
+    y_loop(far, 3)
+
+    def phase2(i, carry):
+        q = block_at(i)
+        for slot in (far, near, home):
+            x_pass(slot, q)
 
         @pl.when(has_ahead)
-        def _(i=i):
+        def _():
             to_tile(far, i).start()
 
-        x_pass(side, q)
-        if i % 2:
-            to_tile(side, i).start()
-        x_pass(near, q)
-        if i % 2 == 0:
-
-            @pl.when(has_behind)
-            def _(i=i):
-                to_tile(near, i).start()
-
-        x_pass(home, q)
-        joined = near if i % 2 else side
+        @pl.when(jnp.logical_and(has_behind, i % 2 == 0))
+        def _():
+            to_tile(near, i).start()
+
+        joined = jnp.where(i % 2 == 1, near, side)
 
         @pl.when(has_behind)
-        def _(i=i, q=q, joined=joined):
+        def _():
             to_tile(diag, i).wait_recv()
             part[joined, q] = part[joined, q] + recv[diag, q]
-            if joined == near:
-                to_tile(near, i).start()
-
-        if joined == side:
-            to_tile(side, i).start()
+
+        @pl.when(jnp.logical_or(has_behind, i % 2 == 0))
+        def _():
+            to_tile(joined, i).start()
+
+        return carry
+
+    lax.fori_loop(0, nq, phase2, 0)
 
     def collect(i):
-        q = blocks[i]
+        q = block_at(i)
         to_tile(side, i).wait_recv()
         part[home, q] = part[home, q] + recv[side, q]
 
@@ -219,9 +242,12 @@
 
     lax.fori_loop(0, all_dates, weigh, 0)
 
-    for i in range(nq - 1):
+    def gather(i, carry):
         collect(i)
-        to_date(blocks[i]).start()
+        to_date(block_at(i)).start()
+        return carry
+
+    lax.fori_loop(0, nq - 1, gather, 0)
 
     rows = bands * rpq
     here = all_dates // nq
@@ -236,7 +262,7 @@
             out_ref[t] = total if first else out_ref[t] + total
             return carry
 
-        lax.fori_loop(0, all_dates, one, 0, unroll=4)
+        lax.fori_loop(0, all_dates, one, 0, unroll=2)
 
     coming = sorted(order[:-1], key=lambda s: order.index(nq - s))
     for n, s in enumerate(coming[:-1]):
@@ -249,20 +275,23 @@
     from_date(q).wait_recv()
     smooth(final.at[q], q, False)
 
-    for i in range(nq):
+    def drain(i, carry):
         to_tile(side, i).wait_send()
 
         @pl.when(has_ahead)
-        def _(i=i):
+        def _():
             to_tile(diag, i).wait_send()
             to_tile(far, i).wait_send()
 
         @pl.when(has_behind)
-        def _(i=i):
+        def _():
             to_tile(near, i).wait_send()
 
+        return carry
+
+    lax.fori_loop(0, nq, drain, 0)
     for i in range(nq - 1):
-        to_date(blocks[i]).wait_send()
+        to_date(block_at(i)).wait_send()
 
 
 def body(granules, coef_x, coef_y, row_offset, col_offset, targets, mask, smoother):

time: 24.3 us -> 25.5 us (1.049); the launches traced: 24.2 us -> 25.1 us
  Pallas kernels: 22.4 us -> 23.4 us
    pallas_call x1, Pallas kernels: 22.4 us -> 23.4 us  [body(): pl.pallas_call(functools.partial(kernel, dims), out_shape=(jax.ShapeDtype...]
where the time goes in v3:
time: 25.5 us; the launch traced here: 25.1 us
  Pallas kernels  23.4 us (92%)
  other arithmetic  1.73 us (7%)
    pallas_call x1, Pallas kernels, body(): pl.pallas_call(functools.partial(kernel, dims), out_shape=(jax.ShapeDtype...  23.4 us
    div x1, other arithmetic, body(): smoothed = numerator / divisor[:, None, :]  1.73 us

profile of v3, /device:TPU:1, one launch (start us, length us, event | category | flops | bytes accessed | tf_op | source)
XLA Modules:
  0.0 25.1 jit_solution(9356486111802306288)
XLA Ops:
  0.0 23.4 %shard_map.82 = (f32[16,40,128]{2,1,0:T(8,128)}, f32[16,128]{1,0:T(8,128)}) custom-call(s32[1,5]{1,0:T(1,128)} %tgt_hbm.1, s32[1,5]{1,0:T(1,128)} %roff_hbm.1, s32[1,5]{1,0:T(1,128)} %coff_hbm.1, s32[1,16]{1,0:T(1,128)} %bitcast.10, f32[16,16]{1,0:T(8,128)} %smoother_hbm.1, bf16[5,12,128]{2,1,0:T(8,128)(2,1)} %bitcast.8, bf16[80,12]{1,0:T(8,128)(2,1)} %bitcast.9, ...), custom_call_target="tpu_custom_call" | custom-call | flops 2000000000 | bytes 4000000 | tf_op jit(solution)/shard_map/pallas_call | solution.py:311
  23.4 1.7 %broadcast_divide_fusion = f32[16,40,128]{2,1,0:T(8,128)} fusion(f32[16,40,128]{2,1,0:T(8,128)} %get-tuple-element.7, f32[16,128]{1,0:T(8,128)} %get-tuple-element.8), kind=kLoop, calls=%fused_computation | loop fusion | flops 81920 | bytes 663552 | tf_op jit(solution)/shard_map/div | solution.py:346

commit v4 on v1

--- a/solution.py
+++ b/solution.py
@@ -9,6 +9,11 @@
 
 MESH = pl.DeviceIdType.MESH
 ROWS = 64
+
+
+def log(size):
+    assert size & (size - 1) == 0
+    return size.bit_length() - 1
 
 
 def kernel(dims, tgt_hbm, roff_hbm, coff_hbm, mask_hbm, smoother_hbm, cx_hbm, cy_hbm, g_hbm, out_ref, divisor_ref,
@@ -61,19 +66,19 @@
     n_e = lax.broadcasted_iota(jnp.int32, (m_count, slots * tile_rows), 1)
 
     def row_of(m):
-        return ((m % per_slot) // (group * rpq)) * rpq + m % rpq
-
-    same_row = row_of(m_e) == n_e % tile_rows
-    slot_e = n_e // tile_rows
-    wanted_e = tile_of(m_e // per_slot)
+        return ((m & (per_slot - 1)) >> log(group * rpq)) * rpq + (m & (rpq - 1))
+
+    same_row = row_of(m_e) == (n_e & (tile_rows - 1))
+    slot_e = n_e >> log(tile_rows)
+    wanted_e = tile_of(m_e >> log(per_slot))
     m = lax.broadcasted_iota(jnp.int32, (m_count, c_count), 0)
     c = lax.broadcasted_iota(jnp.int32, (m_count, c_count), 1)
-    wanted = tile_of(m // per_slot)
+    wanted = tile_of(m >> log(per_slot))
     band_c = jnp.zeros_like(c)
     for b in range(1, group):
         band_c = jnp.where(c >= b * grid_rows, b, band_c)
     base = c - band_c * grid_rows - 2 * row_of(m)
-    base = jnp.where((m // rpq) % group == band_c, base, -1)
+    base = jnp.where(((m >> log(rpq)) & (group - 1)) == band_c, base, -1)
     for copy in small:
         copy.wait()
     aimed = jnp.full_like(n_e, -1)
@@ -148,6 +153,7 @@
     build(diag, 0)
     for step in range(steps):
         fetch(step).wait()
+    for step in range(steps):
         y_pass(diag, 1, step)
     peers = nq + jnp.where(has_ahead, 1, 0) + jnp.where(has_behind, 1, 0)
     pl.semaphore_wait(barrier, peers)

time: 24.3 us -> 23.1 us (0.951)
  Pallas kernels: 22.4 us -> 21.2 us
    pallas_call x1, Pallas kernels: 22.4 us -> 21.2 us  [body(): pl.pallas_call(functools.partial(kernel, dims), out_shape=(jax.ShapeDtype...]
where the time goes in v4:
time: 23.1 us; the launch traced here: 22.9 us
  Pallas kernels  21.2 us (92%)
  other arithmetic  1.73 us (7%)
    pallas_call x1, Pallas kernels, body(): pl.pallas_call(functools.partial(kernel, dims), out_shape=(jax.ShapeDtype...  21.2 us
    div x1, other arithmetic, body(): smoothed = numerator / divisor[:, None, :]  1.73 us

profile of v4, /device:TPU:1, one launch (start us, length us, event | category | flops | bytes accessed | tf_op | source)
XLA Modules:
  0.0 22.9 jit_solution(2638817693595207657)
XLA Ops:
  0.0 21.2 %shard_map.82 = (f32[16,40,128]{2,1,0:T(8,128)}, f32[16,128]{1,0:T(8,128)}) custom-call(s32[1,5]{1,0:T(1,128)} %tgt_hbm.1, s32[1,5]{1,0:T(1,128)} %roff_hbm.1, s32[1,5]{1,0:T(1,128)} %coff_hbm.1, s32[1,16]{1,0:T(1,128)} %bitcast.10, f32[16,16]{1,0:T(8,128)} %smoother_hbm.1, bf16[5,12,128]{2,1,0:T(8,128)(2,1)} %bitcast.8, bf16[80,12]{1,0:T(8,128)(2,1)} %bitcast.9, ...), custom_call_target="tpu_custom_call" | custom-call | flops 2000000000 | bytes 4000000 | tf_op jit(solution)/shard_map/pallas_call | solution.py:288
  21.2 1.7 %broadcast_divide_fusion = f32[16,40,128]{2,1,0:T(8,128)} fusion(f32[16,40,128]{2,1,0:T(8,128)} %get-tuple-element.7, f32[16,128]{1,0:T(8,128)} %get-tuple-element.8), kind=kLoop, calls=%fused_computation | loop fusion | flops 81920 | bytes 663552 | tf_op jit(solution)/shard_map/div | solution.py:323
